TPU v7x, 512 devices: a whole 4x8x8 slice. The times are simulated.
512 devices in a mesh: dom: 64 (over y_lo, z, core), pix: 8 (over x, y_hi).
Axes of the slice: x: 4, y: 8 (y_hi: 2, y_lo: 4; y = y_hi * 4 + y_lo), z: 8, core: 2. Of those that a mesh axis runs over, the one named last changes fastest.
Arguments:
- images: bfloat16 [16384, 16384], P('dom', 'pix'), may hold values from -1500 to 1500
- ctf_group: int32 [16384], P('dom'), may hold values from 0 to 127
- projections: bfloat16 [384, 16384], P('dom', 'pix'), may hold values from -4 to 4
- ctf_table: float32 [128, 16384], P(None, 'pix'), may hold values from 0.1 to 1.5
- noise_power: float32 [16384], P('pix'), may hold values from 1000 to 4000
- prior: float32 [16384], P('pix'), may hold values from 0.01 to 0.1
- log_prior: float32 [16], replicated, may hold values from -3 to 3
- projection_class: int32 [384], replicated, may hold values from 0 to 15, as said below
Outputs:
- class_average: float32 [384, 16384], P('dom', 'pix')
- class_mass: float32 [16], replicated
Inputs may be any that keep to these rules, and one draw needn't show every extreme that they name: `projection_class`: each class names exactly 24 rows.
All inputs are finite; a program needn't handle non-finite values.
Results may differ from a plain program's by a relative error of at most 0.005.
Values may be sent and summed in bfloat16 or wider, within the bound.
A program may use at most 64 MiB of HBM per device.

v0:
```python
import jax
import jax.numpy as jnp
from jax import lax
from jax.sharding import PartitionSpec as P


def posterior(cross_terms, norm_terms, groups, class_bias):
    scores = cross_terms - 0.5 * jnp.take(norm_terms, groups, axis=0) + class_bias[None, :]
    largest = jnp.max(scores, axis=1, keepdims=True)
    raised = jnp.exp(scores - largest)
    return raised / jnp.sum(raised, axis=1, keepdims=True)


def weigh_rows(columns, data):
    return lax.dot_general(
        columns, data, (((0,), (0,)), ((), ())), preferred_element_type=jnp.float32
    )


def body(
    images, ctf_group, projections, ctf_table, noise_power, prior, log_prior, projection_class
):
    part_rows = images.shape[0]
    group_count = ctf_table.shape[0]
    class_count = log_prior.shape[0]
    weight_ctf = ctf_table / noise_power[None, :]
    weight_sq = ctf_table * ctf_table / noise_power[None, :]
    weighted = (images.astype(jnp.float32) * jnp.take(weight_ctf, ctf_group, axis=0)).astype(
        jnp.bfloat16
    )
    class_hot = (
        projection_class[:, None] == jnp.arange(class_count, dtype=jnp.int32)[None, :]
    ).astype(jnp.float32)
    class_bias = jnp.sum(class_hot * log_prior[None, :], axis=1)
    proj_rows = lax.all_gather(projections, "dom", axis=0, tiled=True)
    cross_part = lax.dot_general(
        weighted, proj_rows, (((1,), (1,)), ((), ())), preferred_element_type=jnp.float32
    )
    square = proj_rows.astype(jnp.float32)
    norm_part = lax.dot_general(
        weight_sq,
        square * square,
        (((1,), (1,)), ((), ())),
        precision=lax.Precision.HIGHEST,
        preferred_element_type=jnp.float32,
    )
    cross_terms = cross_part
    norm_terms = norm_part
    cross_terms, norm_terms = lax.psum((cross_terms, norm_terms), "pix")
    membership = posterior(cross_terms, norm_terms, ctf_group, class_bias)
    member_b = membership.astype(jnp.bfloat16)
    local_mass = jnp.sum(jnp.sum(membership, axis=0)[:, None] * class_hot, axis=0)
    class_mass = lax.psum(local_mass, "dom")
    class_mass = class_mass * (class_count / (part_rows * lax.axis_size("dom")))
    group_hot = (ctf_group[:, None] == jnp.arange(group_count, dtype=jnp.int32)[None, :]).astype(
        jnp.bfloat16
    )
    columns = member_b
    weighted_sums = lax.psum_scatter(
        weigh_rows(columns, weighted), "dom", scatter_dimension=0, tiled=True
    )
    columns = member_b
    counts = lax.psum_scatter(
        weigh_rows(columns, group_hot), "dom", scatter_dimension=0, tiled=True
    )
    denominator = (
        jnp.dot(
            counts, weight_sq, precision=lax.Precision.HIGHEST, preferred_element_type=jnp.float32
        )
        + prior[None, :]
    )
    return (weighted_sums / denominator, class_mass)


def solution(mesh):
    placed = (
        P("dom", "pix"),
        P("dom"),
        P("dom", "pix"),
        P(None, "pix"),
        P("pix"),
        P("pix"),
        P(),
        P(),
    )
    return jax.shard_map(
        body, mesh=mesh, in_specs=placed, out_specs=(P("dom", "pix"), P()), check_vma=False
    )
```

profile of v0, /device:TPU:1, one launch (start us, length us, event | category | flops | bytes accessed | tf_op | source)
XLA Modules:
  0.0 929.4 jit_solution(5200808949953770309)
XLA Ops:
  8.6 1.3 broadcast_divide_fusion
  10.0 1.5 gather_fusion
  11.5 1.5 multiply_convert_fusion
  13.0 120.1 %all-gather.3.cloned.1.call-done = bf16[64,6,2048]{2,1,0:T(8,128)(2,1)} async-done(((bf16[1,6,2048]{2,1,0:T(8,128)(2,1)}), bf16[64,6,2048]{2,1,0:T(8,128)(2,1)}) %all-gather.3.cloned.1.call-update) | async-done | bytes 1572880 | tf_op jit(solution)/shard_map/all_gather | solution.py:35
  133.1 2.6 reshape.37
  135.8 5.0 fusion.1
  140.8 1.5 fusion.18
  144.3 112.1 %all-reduce.9.cloned.1.call-done = (f32[256,384]{1,0:T(8,128)}, f32[128,384]{1,0:T(8,128)}) async-done(((f32[256,384]{1,0:T(8,128)}, f32[128,384]{1,0:T(8,128)}), (f32[256,384]{1,0:T(8,128)}, f32[128,384]{1,0:T(8,128)})) %all-reduce.9.cloned.1.call-update) | async-done | bytes 589840 | tf_op jit(solution)/shard_map/psum | solution.py:49
  256.4 2.1 gather_fusion.1
  260.5 163.3 %fusion = f32[8,2048]{1,0:T(8,128)} fusion(f32[384,2048]{1,0:T(8,128)S(1)} %fusion.8), kind=kCustom, calls=%all-reduce-scatter | all-reduce-scatter fusion | flops 1048577 | bytes 3213312
  424.7 2.1 collective-permute-start
  430.7 1.3 collective-permute-start.15
  432.0 1.7 fusion.6
  435.2 1.3 collective-permute-start.13
  436.5 8.0 collective-permute-start.14
  444.5 7.4 collective-permute-start.2
  451.9 6.3 collective-permute-start.3
  458.2 3.4 collective-permute-start.4
  461.7 133.8 %psum.23 = f32[16]{0:T(128)S(1)} all-reduce(f32[16]{0:T(128)S(1)} %select_reduce_fusion), channel_id=1, replica_groups=mesh['dom'=64,'pix'=8] {'dom'}, use_global_device_ids=true, to_apply=%region_9.10 | all-reduce | flops 16 | bytes 128 | tf_op jit(solution)/shard_map/psum | solution.py:53
  596.8 1.3 collective-permute-start.6
  598.1 1.3 collective-permute-start.7
  603.3 2.1 concatenate
  605.4 315.4 %all-reduce.7.cloned.1.call-done = f32[384,128]{1,0:T(8,128)} async-done(((f32[384,128]{1,0:T(8,128)}), f32[384,128]{1,0:T(8,128)}) %all-reduce.7.cloned.1.call-update) | async-done | bytes 196624
  920.8 2.0 dynamic-slice_divide_fusion
  (65 shorter events, 15.7 us)
Async XLA Ops:
  7.2 126.0 %all-gather.3.cloned.1.call-start = ((), (), s32[]{:S(2)}) async-start(), calls=%async_computation | async-start | bytes 2129920 | tf_op jit(solution)/shard_map/all_gather | solution.py:35
  7.9 248.5 %all-reduce.9.cloned.1.call-start = ((), (), s32[]{:S(2)}) async-start(), calls=%async_computation.2 | async-start | bytes 1179648 | tf_op jit(solution)/shard_map/psum | solution.py:49
  13.0 127.7 %copy-start = (bf16[256,2048]{1,0:T(8,128)(2,1)}, bf16[256,2048]{1,0:T(8,128)(2,1)S(1)}, u32[]{:S(2)}) copy-start(bf16[256,2048]{1,0:T(8,128)(2,1)S(1)} %multiply_convert_fusion) | copy-start | bytes 3145732
  13.0 122.7 %copy-start.5 = (f32[2048]{0:T(1024)S(1)}, f32[2048]{0:T(1024)}, u32[]{:S(2)}) copy-start(f32[2048]{0:T(1024)} %param.12) | copy-start | bytes 24580
  142.3 778.5 %all-reduce.7.cloned.1.call-start = ((), (), s32[]{:S(2)}) async-start(), calls=%async_computation.1 | async-start | bytes 393216
  423.8 37.8 %copy-start.7 = (s32[384]{0:T(512)S(1)}, s32[384]{0:T(512)}, u32[]{:S(2)}) copy-start(s32[384]{0:T(512)} %param.15) | copy-start | bytes 4612
  424.7 496.1 %copy-start.2 = (f32[128,2048]{1,0:T(8,128)S(1)}, f32[128,2048]{1,0:T(8,128)}, u32[]{:S(2)}) copy-start(f32[128,2048]{1,0:T(8,128)} %param.11) | copy-start | bytes 3145732
  424.7 496.1 %copy-start.11 = (f32[2048]{0:T(1024)S(1)}, f32[2048]{0:T(1024)}, u32[]{:S(2)}) copy-start(f32[2048]{0:T(1024)} %param.13) | copy-start | bytes 24580
  424.7 10.5 %collective-permute-start = (f32[8,2048]{1,0:T(8,128)}, f32[8,2048]{1,0:T(8,128)S(1)}, u32[]{:S(2)}, u32[]{:S(2)}) collective-permute-start(f32[8,2048]{1,0:T(8,128)} %fusion), channel_id=1, source_target_pairs={{0,8},{8,16},{16,24},{24,32},{32,40},{40,48},{48,56},{56,64},{64,7... | collective-permute-start | bytes 196616
  426.8 9.7 %collective-permute-start.1 = (f32[8,2048]{1,0:T(8,128)}, f32[8,2048]{1,0:T(8,128)S(1)}, u32[]{:S(2)}, u32[]{:S(2)}) collective-permute-start(f32[8,2048]{1,0:T(8,128)} %fusion), channel_id=1, source_target_pairs={{0,16},{8,24},{16,32},{24,40},{32,48},{40,56},{48,64},{56,72},{64,... | collective-permute-start | bytes 196616
  428.1 16.4 %collective-permute-start.10 = (f32[8,2048]{1,0:T(8,128)}, f32[8,2048]{1,0:T(8,128)S(1)}, u32[]{:S(2)}, u32[]{:S(2)}) collective-permute-start(f32[8,2048]{1,0:T(8,128)} %fusion), channel_id=1, source_target_pairs={{0,88},{8,96},{16,104},{24,112},{32,120},{40,128},{48,136},{56,144... | collective-permute-start | bytes 196616
  429.4 22.5 %collective-permute-start.11 = (f32[8,2048]{1,0:T(8,128)}, f32[8,2048]{1,0:T(8,128)S(1)}, u32[]{:S(2)}, u32[]{:S(2)}) collective-permute-start(f32[8,2048]{1,0:T(8,128)} %fusion), channel_id=1, source_target_pairs={{0,96},{8,104},{16,112},{24,120},{32,128},{40,136},{48,144},{56,15... | collective-permute-start | bytes 196616
  430.7 3.0 collective-permute-start.15
  433.7 24.5 %collective-permute-start.12 = (f32[8,2048]{1,0:T(8,128)}, f32[8,2048]{1,0:T(8,128)S(1)}, u32[]{:S(2)}, u32[]{:S(2)}) collective-permute-start(f32[8,2048]{1,0:T(8,128)} %fusion), channel_id=1, source_target_pairs={{0,104},{8,112},{16,120},{24,128},{32,136},{40,144},{48,152},{56,1... | collective-permute-start | bytes 196616
  435.2 160.3 %collective-permute-start.13 = (f32[8,2048]{1,0:T(8,128)S(1)}, f32[8,2048]{1,0:T(8,128)S(1)}, u32[]{:S(2)}, u32[]{:S(2)}) collective-permute-start(f32[8,2048]{1,0:T(8,128)S(1)} %copy-done.3), channel_id=1, source_target_pairs={{0,112},{8,120},{16,128},{24,136},{32,144},{40,152},{48,160},{56,1... | collective-permute-start | bytes 196616
  436.5 160.3 %collective-permute-start.14 = (f32[8,2048]{1,0:T(8,128)S(1)}, f32[8,2048]{1,0:T(8,128)S(1)}, u32[]{:S(2)}, u32[]{:S(2)}) collective-permute-start(f32[8,2048]{1,0:T(8,128)S(1)} %copy-done.3), channel_id=1, source_target_pairs={{0,120},{8,128},{16,136},{24,144},{32,152},{40,160},{48,168},{56,1... | collective-permute-start | bytes 196616
  444.5 153.6 %collective-permute-start.2 = (f32[8,2048]{1,0:T(8,128)S(1)}, f32[8,2048]{1,0:T(8,128)S(1)}, u32[]{:S(2)}, u32[]{:S(2)}) collective-permute-start(f32[8,2048]{1,0:T(8,128)S(1)} %copy-done.3), channel_id=1, source_target_pairs={{0,24},{8,32},{16,40},{24,48},{32,56},{40,64},{48,72},{56,80},{64,... | collective-permute-start | bytes 196616
  451.9 147.5 %collective-permute-start.3 = (f32[8,2048]{1,0:T(8,128)S(1)}, f32[8,2048]{1,0:T(8,128)S(1)}, u32[]{:S(2)}, u32[]{:S(2)}) collective-permute-start(f32[8,2048]{1,0:T(8,128)S(1)} %copy-done.3), channel_id=1, source_target_pairs={{0,32},{8,40},{16,48},{24,56},{32,64},{40,72},{48,80},{56,88},{64,... | collective-permute-start | bytes 196616
  458.2 142.5 %collective-permute-start.4 = (f32[8,2048]{1,0:T(8,128)S(1)}, f32[8,2048]{1,0:T(8,128)S(1)}, u32[]{:S(2)}, u32[]{:S(2)}) collective-permute-start(f32[8,2048]{1,0:T(8,128)S(1)} %copy-done.3), channel_id=1, source_target_pairs={{0,40},{8,48},{16,56},{24,64},{32,72},{40,80},{48,88},{56,96},{64,... | collective-permute-start | bytes 196616
  595.5 7.1 collective-permute-start.5
  596.8 5.8 collective-permute-start.6
  598.1 4.4 collective-permute-start.7
  599.4 3.1 collective-permute-start.8
  600.7 2.6 collective-permute-start.9
  (7 other events, 24.8 us)
Sparse Core Ops, SparseCore 0:
  10.1 122.9 all-gather.2
  142.4 113.9 all-reduce.8
  435.3 485.4 all-reduce.6
where the time goes:
time: 931 us; the launch traced here: 929 us
  waiting for transfers between devices  549 us (59%)
  blocking collectives  297 us (32%)
  starting transfers between devices  41.4 us (4%)
  between operations  15.4 us (2%)
  matrix products  11 us (1%)
  local copies, waits for them, and re-layouts  10.6 us (1%)
    unnamed x20, waiting for transfers between devices  317 us
    unnamed x1, blocking collectives  163 us
    psum x1, blocking collectives, body(): class_mass = lax.psum(local_mass, 'dom')  134 us
    all_gather x1, waiting for transfers between devices, body(): proj_rows = lax.all_gather(projections, 'dom', axis=0, tiled=True)  120 us
    psum x1, waiting for transfers between devices, body(): cross_terms, norm_terms = lax.psum((cross_terms, norm_terms), 'pix')  112 us
    unnamed x17, starting transfers between devices  41.3 us
  transfers between devices with their start and end apart: 19, of which 4 were waited for; matrix products, arithmetic and copies ran while one was open for 1% of the time, Pallas kernels for 0%

commit v1 on v0

v1 whole, which is shorter than its diff:
```python
import functools

import jax
import jax.numpy as jnp
from jax import lax
from jax.experimental import pallas as pl
from jax.experimental.pallas import tpu as pltpu
from jax.sharding import PartitionSpec as P

MESH = pl.DeviceIdType.MESH
F32 = jnp.float32
BF16 = jnp.bfloat16
NZ, NY, NC, NX, NF = 8, 4, 2, 4, 2


def nt(a, b):
    return lax.dot_general(a, b, (((1,), (1,)), ((), ())), preferred_element_type=F32)


def nn(a, b):
    return lax.dot_general(a, b, (((1,), (0,)), ((), ())), preferred_element_type=F32)


def pieces(a, count):
    terms = []
    for _ in range(count):
        term = a.astype(BF16)
        terms.append(term)
        a = a - term.astype(F32)
    return terms


def iota(shape, axis):
    return lax.broadcasted_iota(jnp.int32, shape, axis)


def kernel(
    images_hbm, group_hbm, proj_hbm, ctf_hbm, noise_hbm, prior_hbm, logp_hbm, class_hbm,
    out_ref, mass_ref,
    images, ctf, noise, prior, logp, pclass, group, own_a, own_b,
    ra1, rb1, ra2, rb2, compact_a, compact_b, table3, square2, weighted, hot_t,
    scores, rx, ry, stats, member, s1a, s1b, r1a, r1b, ta, tb, s2a, s2b, r2a, r2b,
    mass_c, mass_z, mass_y,
    load_sem, send_sem, group_sem, w_sem, a1_sem, b1_sem, a2_sem, b2_sem, x_sem, y_sem, st_sem, m_sem,
    p1a_sem, p1b_sem, p2a_sem, p2b_sem, mc_sem, mz_sem, my_sem,
):
    dom, pix = lax.axis_index("dom"), lax.axis_index("pix")
    core, z, y = dom % NC, (dom // NC) % NZ, dom // (NC * NZ)
    x, far = pix // NF, pix % NF
    rows, half = own_a.shape
    parts = images.shape[0]
    groups, pixels = ctf.shape
    zrows = NZ * rows
    yrows = NY * rows
    krows = NY * NZ * rows
    block = NC * parts // NX

    def at_z(o):
        return ((y * NZ + o) * NC + core, pix)

    def at_y(o):
        return ((o * NZ + z) * NC + core, pix)

    def at_x(o):
        return (dom, o * NF + far)

    other_core = ((y * NZ + z) * NC + (1 - core), pix)
    other_far = (dom, x * NF + (1 - far))
    zs = [(z + d) % NZ for d in range(1, NZ)]
    ys = [(y + d) % NY for d in range(1, NY)]
    xs = [(x + d) % NX for d in range(1, NX)]

    sent = []

    def send(src, dst, recv_sem, device):
        copy = pltpu.make_async_remote_copy(
            src_ref=src,
            dst_ref=dst,
            send_sem=send_sem.at[len(sent)],
            recv_sem=recv_sem,
            device_id=device,
            device_id_type=MESH,
        )
        copy.start()
        sent.append(copy)

    def arrived(dst, recv_sem):
        pltpu.make_async_remote_copy(
            src_ref=dst,
            dst_ref=dst,
            send_sem=recv_sem,
            recv_sem=recv_sem,
            device_id=other_core,
            device_id_type=MESH,
        ).wait_recv()

    loads = [
        pltpu.make_async_copy(src, dst, load_sem.at[i])
        for i, (src, dst) in enumerate((
            (proj_hbm.at[:, pl.ds(0, half)], own_a),
            (proj_hbm.at[:, pl.ds(half, half)], own_b),
            (group_hbm, group.at[core]),
            (ctf_hbm, ctf),
            (noise_hbm, noise),
            (images_hbm, images),
            (prior_hbm, prior),
            (logp_hbm, logp),
            (class_hbm, pclass),
        ))
    ]
    for copy in loads:
        copy.start()

    barrier = pltpu.get_barrier_semaphore()
    peers = [at_z(o) for o in zs] + [at_y(o) for o in ys] + [at_x(o) for o in xs]
    peers += [other_core, other_far]
    for peer in peers:
        pl.semaphore_signal(barrier, inc=1, device_id=peer, device_id_type=MESH)
    for copy in loads[:3]:
        copy.wait()
    pl.semaphore_wait(barrier, len(peers))

    for o in zs:
        send(own_a, ra1.at[z], a1_sem.at[z], at_z(o))
    for o in ys:
        send(own_b, rb1.at[y], b1_sem.at[y], at_y(o))
    send(group.at[core], group.at[core], group_sem, other_core)
    ra1[z] = own_a[...]
    rb1[y] = own_b[...]

    for copy in loads[3:]:
        copy.wait()

    def second_a():
        for o in zs:
            arrived(ra1.at[o], a1_sem.at[o])
        for o in range(NZ):
            compact_a[rows * o : rows * (o + 1), :] = ra1[o].astype(F32)
        ra2[y] = compact_a[...].astype(BF16)
        for o in ys:
            send(ra2.at[y], ra2.at[y], a2_sem.at[y], at_y(o))

    def second_b():
        for o in ys:
            arrived(rb1.at[o], b1_sem.at[o])
        for o in zs:
            send(rb1, rb2.at[z], b2_sem.at[z], at_z(o))
        rb2[z] = rb1[...]

    second_b()
    second_a()

    chunk = min(512, half)
    hot_t[:, pl.ds(pl.multiple_of(core * parts, parts), parts)] = (
        iota((groups, parts), 0) == group[core]
    ).astype(BF16)
    own_hot = jnp.transpose((iota((groups, parts), 0) == group[core]).astype(F32)).astype(BF16)
    hot3 = jnp.concatenate([own_hot] * 3, axis=1)
    mine = pl.ds(pl.multiple_of(core * parts, parts), parts)
    for c in range(0, pixels, chunk):
        columns = slice(c, c + chunk)
        table, variance = ctf[:, columns], noise[:, columns]
        for i, term in enumerate(pieces(table / variance, 3)):
            table3[groups * i : groups * (i + 1), columns] = term
        for i, term in enumerate(pieces(table * table / variance, 2)):
            square2[groups * i : groups * (i + 1), columns] = term
        weights = nn(hot3, table3[:, columns])
        weighted[mine, columns] = (images[:, columns].astype(F32) * weights).astype(BF16)
    send(weighted.at[mine], weighted.at[mine], w_sem, other_core)

    owner = ((iota((krows, 1), 0) // rows) * NC + core) * rows + iota((krows, 1), 0) % rows
    picked = iota((krows, NC * krows), 1) == owner
    row_class = jnp.sum(jnp.where(picked, pclass[...], 0), axis=1, keepdims=True)
    class_hot = row_class == iota((krows, logp.shape[1]), 1)
    bias = jnp.sum(jnp.where(class_hot, logp[...], 0.0), axis=1, keepdims=True)

    arrived(group.at[1 - core], group_sem)
    theirs = pl.ds(pl.multiple_of((1 - core) * parts, parts), parts)
    hot_t[:, theirs] = (iota((groups, parts), 0) == group[1 - core]).astype(BF16)

    for o in ys:
        arrived(ra2.at[o], a2_sem.at[o])
    for o in zs:
        arrived(rb2.at[o], b2_sem.at[o])
    for o in range(NZ):
        for p in range(NY):
            first = p * zrows + o * rows
            compact_b[first : first + rows, :] = rb2[o, p].astype(F32)
    proj_a = ra2[...].reshape(krows, half)
    proj_b = compact_b[...].astype(BF16)

    norm2 = jnp.zeros((krows, 2 * groups), F32)
    for proj, columns in ((proj_a, slice(0, half)), (proj_b, slice(half, pixels))):
        wide = proj.astype(F32)
        for term in pieces(wide * wide, 2):
            norm2 += nt(term, square2[:, columns])
    norm = norm2[:, :groups] + norm2[:, groups:]
    norm3 = jnp.concatenate(pieces(norm, 3), axis=1)
    hot_all = hot_t[...]
    norm_n = nn(norm3, jnp.concatenate([hot_all] * 3, axis=0))

    arrived(weighted.at[theirs], w_sem)
    total = nt(proj_a, weighted[:, :half]) + nt(proj_b, weighted[:, half:]) - 0.5 * norm_n
    for o in range(NX):
        scores[o] = total[:, block * o : block * (o + 1)]
    for o in xs:
        send(scores.at[o], rx.at[x], x_sem.at[x], at_x(o))
    rx[x] = scores[x]
    for o in xs:
        arrived(rx.at[o], x_sem.at[o])
    score = rx[0]
    for o in range(1, NX):
        score += rx[o]
    ry[0] = score
    send(ry.at[0], ry.at[1], y_sem, other_far)
    arrived(ry.at[1], y_sem)
    score = ry[0] + ry[1] + bias

    high = jnp.max(score, axis=0, keepdims=True)
    raised = jnp.exp(score - high)
    part = jnp.sum(raised, axis=0, keepdims=True)
    stats[0, 0:1] = high
    stats[0, 1:2] = part
    send(stats.at[0], stats.at[1], st_sem, other_core)
    arrived(stats.at[1], st_sem)
    high_o, part_o = stats[1, 0:1], stats[1, 1:2]
    top = jnp.maximum(high, high_o)
    scale = jnp.exp(high - top)
    scale = scale / (part * scale + part_o * jnp.exp(high_o - top))
    member[x] = (raised * scale).astype(BF16)
    for o in xs:
        send(member.at[x], member.at[x], m_sem.at[x], at_x(o))
    for o in xs:
        arrived(member.at[o], m_sem.at[o])
    members = jnp.concatenate([member[o] for o in range(NX)], axis=1)

    swapped = iota((krows, krows), 0)
    swapped = ((swapped // rows) % NY) * zrows + (swapped // yrows) * rows + swapped % rows
    swap = (iota((krows, krows), 1) == swapped).astype(BF16)
    members_a = nn(swap, members).astype(BF16)
    sums_a = nn(members_a, weighted[:, :half])
    for o in range(NZ):
        s1a[o, :, :half] = sums_a[yrows * o : yrows * (o + 1)].astype(BF16)
    counts = nt(members_a, hot_all)
    for o in range(NZ):
        s1a[o, :, half:] = counts[yrows * o : yrows * (o + 1)].astype(BF16)
    for o in zs:
        send(s1a.at[o], r1a.at[z], p1a_sem.at[z], at_z(o))
    sums_b = nn(members, weighted[:, half:])
    for o in range(NY):
        s1b[o] = sums_b[zrows * o : zrows * (o + 1)].astype(BF16)
    for o in ys:
        send(s1b.at[o], r1b.at[y], p1b_sem.at[y], at_y(o))

    by_row = jnp.sum(members.astype(F32), axis=1, keepdims=True)
    mass = jnp.sum(jnp.where(class_hot, by_row, 0.0), axis=0, keepdims=True)
    mass_c[0] = jnp.broadcast_to(mass, mass_c.shape[1:])
    send(mass_c.at[0], mass_c.at[1], mc_sem, other_core)
    arrived(mass_c.at[1], mc_sem)
    mass_z[z] = mass_c[0] + mass_c[1]
    for o in zs:
        send(mass_z.at[z], mass_z.at[z], mz_sem.at[z], at_z(o))
    for o in zs:
        arrived(mass_z.at[o], mz_sem.at[o])
    mass = mass_z[0]
    for o in range(1, NZ):
        mass += mass_z[o]
    mass_y[y] = mass
    for o in ys:
        send(mass_y.at[y], mass_y.at[y], my_sem.at[y], at_y(o))

    r1b[y] = s1b[y]
    for o in ys:
        arrived(r1b.at[o], p1b_sem.at[o])
    tb[zrows:, :] = jnp.zeros((tb.shape[0] - zrows, half), F32)
    acc = r1b[0].astype(F32)
    for o in range(1, NY):
        acc += r1b[o].astype(F32)
    tb[:zrows, :] = acc
    for o in range(NZ):
        s2b[o] = tb[rows * o : rows * o + 8, :].astype(BF16)
    for o in zs:
        send(s2b.at[o], r2b.at[z], p2b_sem.at[z], at_z(o))

    r1a[z] = s1a[z]
    for o in zs:
        arrived(r1a.at[o], p1a_sem.at[o])
    ta[yrows:, :] = jnp.zeros((ta.shape[0] - yrows, ta.shape[1]), F32)
    acc = r1a[0].astype(F32)
    for o in range(1, NZ):
        acc += r1a[o].astype(F32)
    ta[:yrows, :] = acc
    for o in range(NY):
        s2a[o] = ta[rows * o : rows * o + 8, :].astype(BF16)
    for o in ys:
        send(s2a.at[o], r2a.at[y], p2a_sem.at[y], at_y(o))

    for o in ys:
        arrived(mass_y.at[o], my_sem.at[o])
    mass = mass_y[0]
    for o in range(1, NY):
        mass += mass_y[o]
    mass_ref[...] = mass[0:1] * (logp.shape[1] / (parts * NZ * NY * NC))

    r2a[y] = s2a[y]
    for o in ys:
        arrived(r2a.at[o], p2a_sem.at[o])
    acc = r2a[0].astype(F32)
    for o in range(1, NY):
        acc += r2a[o].astype(F32)
    denominator = prior[...]
    for term in pieces(acc[:, half:], 3):
        denominator = denominator + nn(jnp.concatenate([term, term], axis=1), square2[...])
    out_ref[:, :half] = (acc[:, :half] / denominator[:, :half])[:rows]
    r2b[z] = s2b[z]
    for o in zs:
        arrived(r2b.at[o], p2b_sem.at[o])
    acc = r2b[0].astype(F32)
    for o in range(1, NZ):
        acc += r2b[o].astype(F32)
    out_ref[:, half:] = (acc / denominator[:, half:])[:rows]

    for copy in sent:
        copy.wait_send()


SENDS = 2 * (5 * (NZ - 1) + 5 * (NY - 1) + 2 * (NX - 1) + 6)


def body(images, ctf_group, projections, ctf_table, noise_power, prior, log_prior, projection_class):
    parts, pixels = images.shape
    groups = ctf_table.shape[0]
    classes = log_prior.shape[0]
    rows = projections.shape[0]
    half = pixels // 2
    krows = NZ * NY * rows
    zrows, yrows = NZ * rows, NY * rows
    chip = NC * parts
    block = chip // NX
    pad = 8

    def up(n):
        return -(-n // pad) * pad

    vmem = pltpu.VMEM
    dma = pltpu.SemaphoreType.DMA
    sums, mass = pl.pallas_call(
        kernel,
        out_shape=(
            jax.ShapeDtypeStruct((rows, pixels), F32),
            jax.ShapeDtypeStruct((1, classes), F32),
        ),
        in_specs=[pl.BlockSpec(memory_space=pl.ANY)] * 8,
        out_specs=[pl.BlockSpec(memory_space=pltpu.VMEM)] * 2,
        scratch_shapes=[
            vmem((parts, pixels), BF16),
            vmem((groups, pixels), F32),
            vmem((1, pixels), F32),
            vmem((1, pixels), F32),
            vmem((1, classes), F32),
            vmem((1, NC * krows), jnp.int32),
            vmem((NC, 1, parts), jnp.int32),
            vmem((rows, half), BF16),
            vmem((rows, half), BF16),
            vmem((NZ, rows, half), BF16),
            vmem((NY, rows, half), BF16),
            vmem((NY, zrows, half), BF16),
            vmem((NZ, NY, rows, half), BF16),
            vmem((zrows, half), F32),
            vmem((krows, half), F32),
            vmem((3 * groups, pixels), BF16),
            vmem((2 * groups, pixels), BF16),
            vmem((chip, pixels), BF16),
            vmem((groups, chip), BF16),
            vmem((NX, krows, block), F32),
            vmem((NX, krows, block), F32),
            vmem((2, krows, block), F32),
            vmem((2, 8, block), F32),
            vmem((NX, krows, block), BF16),
            vmem((NZ, yrows, half + groups), BF16),
            vmem((NY, zrows, half), BF16),
            vmem((NZ, yrows, half + groups), BF16),
            vmem((NY, zrows, half), BF16),
            vmem((up(rows * (NY - 1) + 8), half + groups), F32),
            vmem((up(rows * (NZ - 1) + 8), half), F32),
            vmem((NY, 8, half + groups), BF16),
            vmem((NZ, 8, half), BF16),
            vmem((NY, 8, half + groups), BF16),
            vmem((NZ, 8, half), BF16),
            vmem((2, 8, classes), F32),
            vmem((NZ, 8, classes), F32),
            vmem((NY, 8, classes), F32),
            dma((9,)),
            dma((SENDS,)),
            dma, dma,
            dma((NZ,)), dma((NY,)), dma((NY,)), dma((NZ,)),
            dma((NX,)), dma, dma, dma((NX,)),
            dma((NZ,)), dma((NY,)), dma((NY,)), dma((NZ,)),
            dma, dma((NZ,)), dma((NY,)),
        ],
        compiler_params=pltpu.CompilerParams(
            collective_id=0, has_side_effects=True, vmem_limit_bytes=56 * 1024 * 1024
        ),
        cost_estimate=pl.CostEstimate(
            flops=4 * chip * krows * pixels, bytes_accessed=4 * parts * pixels, transcendentals=krows * block
        ),
    )(
        images,
        ctf_group.reshape(1, parts),
        projections,
        ctf_table,
        noise_power.reshape(1, pixels),
        prior.reshape(1, pixels),
        log_prior.reshape(1, classes),
        projection_class.reshape(1, NC * krows),
    )
    return sums, mass.reshape(classes)


def solution(mesh):
    placed = (
        P("dom", "pix"),
        P("dom"),
        P("dom", "pix"),
        P(None, "pix"),
        P("pix"),
        P("pix"),
        P(),
        P(),
    )
    return jax.shard_map(
        body, mesh=mesh, in_specs=placed, out_specs=(P("dom", "pix"), P()), check_vma=False
    )
```

time: 931 us -> 77.9 us (0.08)
  waiting for transfers between devices: 549 us -> 0 us
  blocking collectives: 297 us -> 0 us
  Pallas kernels: 0 us -> 73.8 us
  starting transfers between devices: 41.4 us -> 0 us
  between operations: 15.4 us -> 0.66 us
  matrix products: 11 us -> 0 us
    unnamed x20 -> x0, waiting for transfers between devices: 317 us -> none
    unnamed x1 -> x0, blocking collectives: 163 us -> none
    psum x1 -> x0, blocking collectives: 134 us -> none  [body(): class_mass = lax.psum(local_mass, 'dom')]
    all_gather x1 -> x0, waiting for transfers between devices: 120 us -> none  [body(): proj_rows = lax.all_gather(projections, 'dom', axis=0, tiled=True)]
    psum x1 -> x0, waiting for transfers between devices: 112 us -> none  [body(): cross_terms, norm_terms = lax.psum((cross_terms, norm_terms), 'pix')]
    pallas_call x0 -> x1, Pallas kernels: none -> 73.8 us  [body(): pl.pallas_call(kernel, out_shape=(jax.ShapeDtypeStruct((rows, pixels), F3...]
    unnamed x17 -> x0, starting transfers between devices: 41.3 us -> none
    dot_general x5 -> x0, matrix products: 11 us -> none  [the longest x1 5 us: body(): lax.dot_general(weight_sq, square * square, (((1,), (1,)), ((), ())), pre...]
  transfers between devices with their start and end apart: 19 -> 0, of which waited for: 4 -> 0; matrix products, arithmetic and copies ran while one was open for 1% -> 0% of each run, Pallas kernels for 0% -> 0%
where the time goes in v1:
time: 77.9 us; the launch traced here: 77.7 us
  Pallas kernels  73.8 us (95%)
  local copies, waits for them, and re-layouts  3.23 us (4%)
    pallas_call x1, Pallas kernels, body(): pl.pallas_call(kernel, out_shape=(jax.ShapeDtypeStruct((rows, pixels), F3...  73.8 us
    unnamed x6, local copies, waits for them, and re-layouts  2.66 us

profile of v1, /device:TPU:1, one launch (start us, length us, event | category | flops | bytes accessed | tf_op | source)
XLA Modules:
  0.0 77.7 jit_solution(14849747826965674842)
XLA Ops:
  0.6 0.0 copy-start
  0.6 0.7 copy-done
  1.3 0.6 reshape.26.class_hbm
  1.9 73.8 %shard_map.95 = (f32[6,2048]{1,0:T(8,128)}, f32[1,16]{1,0:T(1,128)}) custom-call(bf16[256,2048]{1,0:T(8,128)(2,1)} %images_hbm.1, s32[1,256]{1,0:T(1,128)} %bitcast.7, bf16[6,2048]{1,0:T(8,128)(2,1)} %proj_hbm.1, f32[128,2048]{1,0:T(8,128)} %ctf_hbm.1, f32[1,2048]{1,0:T(1,128)} %bitcast.5, f32[1,2048]{1,0:T(1,128)} %bitcast.6, f32[1,16]{1,0:T(1,128)} %bitcast.8, ...), custom_call_target="tpu_custom_call" | custom-call | flops 805306368 | bytes 2097152 | tf_op jit(solution)/shard_map/pallas_call | solution.py:347
  75.7 0.0 copy-start.1
  75.7 1.5 %copy.12 = f32[6,2048]{1,0:T(8,128)} copy(f32[6,2048]{1,0:T(8,128)} %get-tuple-element.8) | data formatting | bytes 98304
  77.1 0.0 copy-done.1
  77.2 0.5 copy.13
Async XLA Ops:
  0.6 0.7 copy-start
  75.7 1.5 %copy-start.1 = (f32[1,16]{1,0:T(1,128)S(1)}, f32[1,16]{1,0:T(1,128)}, u32[]{:S(2)}) copy-start(f32[1,16]{1,0:T(1,128)} %get-tuple-element.5) | copy-start | bytes 196

commit v2 on v1

v2 whole, which is shorter than its diff:
```python
import functools

import jax
import jax.numpy as jnp
from jax import lax
from jax.experimental import pallas as pl
from jax.experimental.pallas import tpu as pltpu
from jax.sharding import PartitionSpec as P

MESH = pl.DeviceIdType.MESH
F32 = jnp.float32
BF16 = jnp.bfloat16
NZ, NY, NC, NX, NF = 8, 4, 2, 4, 2
GATHER_Z, SUM_Z = 1024, 768
STEPS = 2


def nt(a, b):
    return lax.dot_general(a, b, (((1,), (1,)), ((), ())), preferred_element_type=F32)


def nn(a, b):
    return lax.dot_general(a, b, (((1,), (0,)), ((), ())), preferred_element_type=F32)


def pieces(a, count):
    terms = []
    for _ in range(count):
        term = a.astype(BF16)
        terms.append(term)
        a = a - term.astype(F32)
    return terms


def iota(shape, axis):
    return lax.broadcasted_iota(jnp.int32, shape, axis)


def kernel(
    images_hbm, group_hbm, proj_hbm, ctf_hbm, noise_hbm, prior_hbm, logp_hbm, class_hbm,
    out_ref, mass_ref,
    images, ctf, noise, prior, logp, pclass, group, own_a, own_b,
    ra1, rb1, ra2, rb2, compact_a, compact_b, table3, square2, weighted, hot_t,
    scores, rx, ry, stats, member, s1a, s1b, r1a, r1b, ta, tb, s2a, s2b, r2a, r2b,
    mass_c, mass_z, mass_y,
    load_sem, send_sem, group_sem, w_sem, a1_sem, b1_sem, a2_sem, b2_sem, x_sem, y_sem, st_sem, m_sem,
    p1a_sem, p1b_sem, p2a_sem, p2b_sem, mc_sem, mz_sem, my_sem,
):
    dom, pix = lax.axis_index("dom"), lax.axis_index("pix")
    core, z, y = dom % NC, (dom // NC) % NZ, dom // (NC * NZ)
    x, far = pix // NF, pix % NF
    rows, cut = own_a.shape
    parts = images.shape[0]
    groups, pixels = ctf.shape
    first_z = s1a.shape[2] - groups
    zrows = NZ * rows
    yrows = NY * rows
    krows = NY * NZ * rows
    block = NC * parts // NX

    def at_z(o):
        return ((y * NZ + o) * NC + core, pix)

    def at_y(o):
        return ((o * NZ + z) * NC + core, pix)

    def at_x(o):
        return (dom, o * NF + far)

    other_core = ((y * NZ + z) * NC + (1 - core), pix)
    other_far = (dom, x * NF + (1 - far))
    zs = [(z + d) % NZ for d in (4, 3, 5, 2, 6, 1, 7)[8 - NZ :]]
    ys = [(y + d) % NY for d in (2, 1, 3)[4 - NY :]]
    xs = [(x + d) % NX for d in (2, 1, 3)[4 - NX :]]

    sent = []

    def send(src, dst, recv_sem, device):
        copy = pltpu.make_async_remote_copy(
            src_ref=src,
            dst_ref=dst,
            send_sem=send_sem.at[len(sent)],
            recv_sem=recv_sem,
            device_id=device,
            device_id_type=MESH,
        )
        copy.start()
        sent.append(copy)

    def arrived(dst, recv_sem):
        pltpu.make_async_remote_copy(
            src_ref=dst,
            dst_ref=dst,
            send_sem=recv_sem,
            recv_sem=recv_sem,
            device_id=other_core,
            device_id_type=MESH,
        ).wait_recv()

    loads = [
        pltpu.make_async_copy(src, dst, load_sem.at[i])
        for i, (src, dst) in enumerate((
            (proj_hbm.at[:, pl.ds(0, cut)], own_a),
            (proj_hbm.at[:, pl.ds(cut, pixels - cut)], own_b),
            (group_hbm, group.at[core]),
            (ctf_hbm, ctf),
            (noise_hbm, noise),
            (images_hbm, images),
            (prior_hbm, prior),
            (logp_hbm, logp),
            (class_hbm, pclass),
        ))
    ]
    for copy in loads:
        copy.start()

    barrier = pltpu.get_barrier_semaphore()
    peers = [at_z(o) for o in zs] + [at_y(o) for o in ys] + [at_x(o) for o in xs]
    peers += [other_core, other_far]
    for peer in peers:
        pl.semaphore_signal(barrier, inc=1, device_id=peer, device_id_type=MESH)
    for copy in loads[:3]:
        copy.wait()
    pl.semaphore_wait(barrier, len(peers))

    for o in zs:
        send(own_a, ra1.at[z], a1_sem.at[z], at_z(o))
    for o in ys:
        send(own_b, rb1.at[y], b1_sem.at[y], at_y(o))
    send(group.at[core], group.at[core], group_sem, other_core)
    ra1[z] = own_a[...]
    rb1[y] = own_b[...]

    for copy in loads[3:]:
        copy.wait()

    def second_a():
        for o in zs:
            arrived(ra1.at[o], a1_sem.at[o])
        for o in range(NZ):
            compact_a[rows * o : rows * (o + 1), :] = ra1[o].astype(F32)
        ra2[y] = compact_a[...].astype(BF16)
        for o in ys:
            send(ra2.at[y], ra2.at[y], a2_sem.at[y], at_y(o))

    def second_b():
        for o in ys:
            arrived(rb1.at[o], b1_sem.at[o])
        for o in range(NY):
            compact_b[rows * o : rows * (o + 1), :] = rb1[o].astype(F32)
        rb2[z] = compact_b[:yrows, :].astype(BF16)
        for o in zs:
            send(rb2.at[z], rb2.at[z], b2_sem.at[z], at_z(o))

    second_b()
    second_a()

    chunk = min(512, pixels)
    own_hot = jnp.transpose((iota((groups, parts), 0) == group[core]).astype(F32)).astype(BF16)
    hot3 = jnp.concatenate([own_hot] * 3, axis=1)
    mine = pl.ds(pl.multiple_of(core * parts, parts), parts)
    for c in range(0, pixels, chunk):
        columns = slice(c, c + chunk)
        table, variance = ctf[:, columns], noise[:, columns]
        for i, term in enumerate(pieces(table / variance, 3)):
            table3[groups * i : groups * (i + 1), columns] = term
        for i, term in enumerate(pieces(table * table / variance, 2)):
            square2[groups * i : groups * (i + 1), columns] = term
        weights = nn(hot3, table3[:, columns])
        weighted[mine, columns] = (images[:, columns].astype(F32) * weights).astype(BF16)
    send(weighted.at[mine], weighted.at[mine], w_sem, other_core)
    theirs = pl.ds(pl.multiple_of((1 - core) * parts, parts), parts)

    owner = ((iota((krows, 1), 0) // rows) * NC + core) * rows + iota((krows, 1), 0) % rows
    picked = iota((krows, NC * krows), 1) == owner
    row_class = jnp.sum(jnp.where(picked, pclass[...].reshape(1, NC * krows), 0), axis=1, keepdims=True)
    class_hot = row_class == iota((krows, logp.shape[1]), 1)
    bias = jnp.sum(jnp.where(class_hot, logp[...], 0.0), axis=1, keepdims=True)

    arrived(group.at[1 - core], group_sem)
    for o in range(NX):
        first = o * block % parts
        hot_t[o] = (iota((groups, block), 0) == group[o * block // parts, :, first : first + block]).astype(BF16)

    arrived(weighted.at[theirs], w_sem)

    def squares(proj, columns):
        wide = proj.astype(F32)
        high, low = pieces(wide * wide, 2)
        return nt(high, square2[:, columns]) + nt(low, square2[:, columns])

    for o in ys:
        arrived(ra2.at[o], a2_sem.at[o])
    proj_a = ra2[...].reshape(krows, cut)
    cross = nt(proj_a, weighted[:, :cut])
    for h in range(STEPS):
        some = slice(krows // STEPS * h, krows // STEPS * (h + 1))
        for o in range(NX):
            scores[h, o] = cross[some, block * o : block * (o + 1)]
    norm_a = squares(proj_a, slice(0, cut))

    for o in zs:
        arrived(rb2.at[o], b2_sem.at[o])
    for o in range(NZ):
        wide = rb2[o].astype(F32)
        for p in range(NY):
            first = p * zrows + o * rows
            compact_b[first : first + rows, :] = wide[rows * p : rows * (p + 1)]
    proj_b = compact_b[...].astype(BF16)
    norm2 = norm_a + squares(proj_b, slice(cut, pixels))
    norm = norm2[:, :groups] + norm2[:, groups:]
    norm3 = jnp.concatenate([term for term in pieces(-0.5 * norm, 3)], axis=1)
    part = krows // STEPS
    for h in range(STEPS):
        some = slice(part * h, part * (h + 1))
        for o in [*xs, x]:
            these = pl.ds(pl.multiple_of(o * block, block), block)
            hot3 = jnp.concatenate([hot_t[o]] * 3, axis=0)
            scores[h, o] += nt(proj_b[some], weighted[these, cut:]) + nn(norm3[some], hot3)
            if o is not x:
                send(scores.at[h, o], rx.at[h, x], x_sem.at[h, x], at_x(o))
    for h in range(STEPS):
        for o in xs:
            arrived(rx.at[h, o], x_sem.at[h, o])
        score = scores[h, x]
        for o in xs:
            score += rx[h, o]
        ry[h, 0] = score
        send(ry.at[h, 0], ry.at[h, 1], y_sem.at[h], other_far)
    for h in range(STEPS):
        arrived(ry.at[h, 1], y_sem.at[h])
    score = jnp.concatenate([ry[h, 0] + ry[h, 1] for h in range(STEPS)], axis=0) + bias

    high = jnp.max(score, axis=0, keepdims=True)
    raised = jnp.exp(score - high)
    part = jnp.sum(raised, axis=0, keepdims=True)
    stats[0, 0:1] = high
    stats[0, 1:2] = part
    send(stats.at[0], stats.at[1], st_sem, other_core)
    arrived(stats.at[1], st_sem)
    high_o, part_o = stats[1, 0:1], stats[1, 1:2]
    top = jnp.maximum(high, high_o)
    scale = jnp.exp(high - top)
    scale = scale / (part * scale + part_o * jnp.exp(high_o - top))
    member[x] = (raised * scale).astype(BF16)
    for o in xs:
        send(member.at[x], member.at[x], m_sem.at[x], at_x(o))
    for o in xs:
        arrived(member.at[o], m_sem.at[o])
    members = jnp.concatenate([member[o] for o in range(NX)], axis=1)

    def first_sum_b(h):
        columns = slice(first_z + width * h, first_z + width * (h + 1))
        sums = nn(members, weighted[:, columns])
        for o in range(NY):
            s1b[h, o] = sums[zrows * o : zrows * (o + 1)].astype(BF16)
        for o in ys:
            send(s1b.at[h, o], r1b.at[h, y], p1b_sem.at[h, y], at_y(o))

    width = s1b.shape[3]
    first_sum_b(0)

    swapped = iota((krows, krows), 0)
    swapped = ((swapped // rows) % NY) * zrows + (swapped // yrows) * rows + swapped % rows
    swap = (iota((krows, krows), 1) == swapped).astype(BF16)
    members_z = nn(swap, members).astype(BF16)
    hot_all = jnp.concatenate([hot_t[o] for o in range(NX)], axis=1)
    counts = nt(members_z, hot_all)
    sums = nn(members_z, weighted[:, :first_z])
    for o in range(NZ):
        s1a[o, :, :first_z] = sums[yrows * o : yrows * (o + 1)].astype(BF16)
        s1a[o, :, first_z:] = counts[yrows * o : yrows * (o + 1)].astype(BF16)
    for o in zs:
        send(s1a.at[o], r1a.at[z], p1a_sem.at[z], at_z(o))

    for h in range(1, STEPS):
        first_sum_b(h)

    by_row = jnp.sum(members.astype(F32), axis=1, keepdims=True)
    mass = jnp.sum(jnp.where(class_hot, by_row, 0.0), axis=0, keepdims=True)
    mass_z[z] = jnp.broadcast_to(mass, mass_z.shape[1:])
    for o in zs:
        send(mass_z.at[z], mass_z.at[z], mz_sem.at[z], at_z(o))

    tb[zrows:, :] = jnp.zeros((tb.shape[0] - zrows, tb.shape[1]), F32)
    ta[yrows:, :] = jnp.zeros((ta.shape[0] - yrows, ta.shape[1]), F32)

    def second_sum_b(h):
        for o in ys:
            arrived(r1b.at[h, o], p1b_sem.at[h, o])
        acc = s1b[h, y].astype(F32)
        for o in ys:
            acc += r1b[h, o].astype(F32)
        tb[:zrows, :] = acc
        for o in range(NZ):
            s2b[h, o] = tb[rows * o : rows * o + 8, :].astype(BF16)
        for o in zs:
            send(s2b.at[h, o], r2b.at[h, z], p2b_sem.at[h, z], at_z(o))

    def second_sum_a():
        for o in zs:
            arrived(r1a.at[o], p1a_sem.at[o])
        acc = s1a[z].astype(F32)
        for o in zs:
            acc += r1a[o].astype(F32)
        ta[:yrows, :] = acc
        for o in range(NY):
            s2a[o] = ta[rows * o : rows * o + 8, :].astype(BF16)
        for o in ys:
            send(s2a.at[o], r2a.at[y], p2a_sem.at[y], at_y(o))

    second_sum_b(0)
    second_sum_a()
    for h in range(1, STEPS):
        second_sum_b(h)

    for o in zs:
        arrived(mass_z.at[o], mz_sem.at[o])
    mass = mass_z[0]
    for o in range(1, NZ):
        mass += mass_z[o]
    mass_y[y] = mass
    for o in ys:
        send(mass_y.at[y], mass_y.at[y], my_sem.at[y], at_y(o))

    for o in ys:
        arrived(r2a.at[o], p2a_sem.at[o])
    acc = s2a[y].astype(F32)
    for o in ys:
        acc += r2a[o].astype(F32)
    counted = jnp.concatenate([term.astype(F32) for term in pieces(acc[:, first_z:], 3)], axis=0).astype(BF16)
    filtered = nn(jnp.concatenate([counted, counted], axis=1), square2[...])
    denominator = filtered[0:8] + filtered[8:16] + filtered[16:24] + prior[...]
    out_ref[:, :first_z] = (acc[:, :first_z] / denominator[:, :first_z])[:rows]
    inverse = 1.0 / denominator[:, first_z:]

    for o in ys:
        arrived(mass_y.at[o], my_sem.at[o])
    mass = mass_y[0]
    for o in range(1, NY):
        mass += mass_y[o]
    mass_c[0] = mass
    send(mass_c.at[0], mass_c.at[1], mc_sem, other_core)
    arrived(mass_c.at[1], mc_sem)
    mass_ref[...] = (mass_c[0] + mass_c[1])[0:1] * (logp.shape[1] / (parts * NZ * NY * NC))

    for h in range(STEPS):
        for o in zs:
            arrived(r2b.at[h, o], p2b_sem.at[h, o])
        acc = s2b[h, z].astype(F32)
        for o in zs:
            acc += r2b[h, o].astype(F32)
        columns = slice(width * h, width * (h + 1))
        out_ref[:, first_z + width * h : first_z + width * (h + 1)] = (acc * inverse[:, columns])[:rows]

    for copy in sent:
        copy.wait_send()


SENDS = STEPS * (5 * (NZ - 1) + 5 * (NY - 1) + 2 * (NX - 1) + 6)


def body(images, ctf_group, projections, ctf_table, noise_power, prior, log_prior, projection_class):
    parts, pixels = images.shape
    groups = ctf_table.shape[0]
    classes = log_prior.shape[0]
    rows = projections.shape[0]
    cut, first_z = GATHER_Z, SUM_Z
    width = (pixels - first_z) // STEPS
    krows = NZ * NY * rows
    zrows, yrows = NZ * rows, NY * rows
    chip = NC * parts
    block = chip // NX
    pad = 8

    def up(n):
        return -(-n // pad) * pad

    vmem = pltpu.VMEM
    dma = pltpu.SemaphoreType.DMA
    sums, mass = pl.pallas_call(
        kernel,
        out_shape=(
            jax.ShapeDtypeStruct((rows, pixels), F32),
            jax.ShapeDtypeStruct((1, classes), F32),
        ),
        in_specs=[pl.BlockSpec(memory_space=pl.ANY)] * 8,
        out_specs=[pl.BlockSpec(memory_space=pltpu.VMEM)] * 2,
        scratch_shapes=[
            vmem((parts, pixels), BF16),
            vmem((groups, pixels), F32),
            vmem((1, pixels), F32),
            vmem((1, pixels), F32),
            vmem((1, classes), F32),
            vmem((NC * krows,), jnp.int32),
            vmem((NC, 1, parts), jnp.int32),
            vmem((rows, cut), BF16),
            vmem((rows, pixels - cut), BF16),
            vmem((NZ, rows, cut), BF16),
            vmem((NY, rows, pixels - cut), BF16),
            vmem((NY, zrows, cut), BF16),
            vmem((NZ, yrows, pixels - cut), BF16),
            vmem((zrows, cut), F32),
            vmem((krows, pixels - cut), F32),
            vmem((3 * groups, pixels), BF16),
            vmem((2 * groups, pixels), BF16),
            vmem((chip, pixels), BF16),
            vmem((NX, groups, block), BF16),
            vmem((STEPS, NX, krows // STEPS, block), F32),
            vmem((STEPS, NX, krows // STEPS, block), F32),
            vmem((STEPS, 2, krows // STEPS, block), F32),
            vmem((2, 8, block), F32),
            vmem((NX, krows, block), BF16),
            vmem((NZ, yrows, first_z + groups), BF16),
            vmem((STEPS, NY, zrows, width), BF16),
            vmem((NZ, yrows, first_z + groups), BF16),
            vmem((STEPS, NY, zrows, width), BF16),
            vmem((up(rows * (NY - 1) + 8), first_z + groups), F32),
            vmem((up(rows * (NZ - 1) + 8), width), F32),
            vmem((NY, 8, first_z + groups), BF16),
            vmem((STEPS, NZ, 8, width), BF16),
            vmem((NY, 8, first_z + groups), BF16),
            vmem((STEPS, NZ, 8, width), BF16),
            vmem((2, 8, classes), F32),
            vmem((NZ, 8, classes), F32),
            vmem((NY, 8, classes), F32),
            dma((9,)),
            dma((SENDS,)),
            dma, dma,
            dma((NZ,)), dma((NY,)), dma((NY,)), dma((NZ,)),
            dma((STEPS, NX)), dma((STEPS,)), dma, dma((NX,)),
            dma((NZ,)), dma((STEPS, NY)), dma((NY,)), dma((STEPS, NZ)),
            dma, dma((NZ,)), dma((NY,)),
        ],
        compiler_params=pltpu.CompilerParams(
            collective_id=0, has_side_effects=True, vmem_limit_bytes=56 * 1024 * 1024
        ),
        cost_estimate=pl.CostEstimate(
            flops=4 * chip * krows * pixels, bytes_accessed=4 * parts * pixels, transcendentals=krows * block
        ),
    )(
        images,
        ctf_group.reshape(1, parts),
        projections,
        ctf_table,
        noise_power.reshape(1, pixels),
        prior.reshape(1, pixels),
        log_prior.reshape(1, classes),
        projection_class,
    )
    return sums, mass.reshape(classes)


def solution(mesh):
    placed = (
        P("dom", "pix"),
        P("dom"),
        P("dom", "pix"),
        P(None, "pix"),
        P("pix"),
        P("pix"),
        P(),
        P(),
    )
    return jax.shard_map(
        body, mesh=mesh, in_specs=placed, out_specs=(P("dom", "pix"), P()), check_vma=False
    )
```

time: 77.9 us -> 70.5 us (0.905)
  Pallas kernels: 73.8 us -> 67.6 us
  local copies, waits for them, and re-layouts: 3.23 us -> 1.99 us
    pallas_call x1, Pallas kernels: 73.8 us -> 67.6 us  [body(): pl.pallas_call(kernel, out_shape=(jax.ShapeDtypeStruct((rows, pixels), F3...]
    unnamed x6 -> x4, local copies, waits for them, and re-layouts: 2.66 us -> 1.99 us
where the time goes in v2:
time: 70.5 us; the launch traced here: 70.3 us
  Pallas kernels  67.6 us (96%)
  local copies, waits for them, and re-layouts  1.99 us (3%)
    pallas_call x1, Pallas kernels, body(): pl.pallas_call(kernel, out_shape=(jax.ShapeDtypeStruct((rows, pixels), F3...  67.6 us
    unnamed x4, local copies, waits for them, and re-layouts  1.99 us

profile of v2, /device:TPU:1, one launch (start us, length us, event | category | flops | bytes accessed | tf_op | source)
XLA Modules:
  0.0 70.3 jit_solution(14584522554108625687)
XLA Ops:
  0.6 67.6 %shard_map.95 = (f32[6,2048]{1,0:T(8,128)}, f32[1,16]{1,0:T(1,128)}) custom-call(bf16[256,2048]{1,0:T(8,128)(2,1)} %images_hbm.1, s32[1,256]{1,0:T(1,128)} %bitcast.7, bf16[6,2048]{1,0:T(8,128)(2,1)} %proj_hbm.1, f32[128,2048]{1,0:T(8,128)} %ctf_hbm.1, f32[1,2048]{1,0:T(1,128)} %bitcast.5, f32[1,2048]{1,0:T(1,128)} %bitcast.6, f32[1,16]{1,0:T(1,128)} %bitcast.8, ...), custom_call_target="tpu_custom_call" | custom-call | flops 805306368 | bytes 2097152 | tf_op jit(solution)/shard_map/pallas_call | solution.py:381
  68.3 0.0 copy-start
  68.3 1.5 %copy.12 = f32[6,2048]{1,0:T(8,128)} copy(f32[6,2048]{1,0:T(8,128)} %get-tuple-element.8) | data formatting | bytes 98304
  69.8 0.0 copy-done
  69.8 0.5 copy.13
Async XLA Ops:
  68.3 1.5 %copy-start = (f32[1,16]{1,0:T(1,128)S(1)}, f32[1,16]{1,0:T(1,128)}, u32[]{:S(2)}) copy-start(f32[1,16]{1,0:T(1,128)} %get-tuple-element.5) | copy-start | bytes 196

commit v3 on v2

--- a/solution.py
+++ b/solution.py
@@ -12,7 +12,7 @@
 BF16 = jnp.bfloat16
 NZ, NY, NC, NX, NF = 8, 4, 2, 4, 2
 GATHER_Z, SUM_Z = 1024, 768
-STEPS = 2
+SCORE_STEPS, SUM_STEPS = 2, 2
 
 
 def nt(a, b):
@@ -193,8 +193,8 @@
         arrived(ra2.at[o], a2_sem.at[o])
     proj_a = ra2[...].reshape(krows, cut)
     cross = nt(proj_a, weighted[:, :cut])
-    for h in range(STEPS):
-        some = slice(krows // STEPS * h, krows // STEPS * (h + 1))
+    for h in range(SCORE_STEPS):
+        some = slice(krows // SCORE_STEPS * h, krows // SCORE_STEPS * (h + 1))
         for o in range(NX):
             scores[h, o] = cross[some, block * o : block * (o + 1)]
     norm_a = squares(proj_a, slice(0, cut))
@@ -210,8 +210,8 @@
     norm2 = norm_a + squares(proj_b, slice(cut, pixels))
     norm = norm2[:, :groups] + norm2[:, groups:]
     norm3 = jnp.concatenate([term for term in pieces(-0.5 * norm, 3)], axis=1)
-    part = krows // STEPS
-    for h in range(STEPS):
+    part = krows // SCORE_STEPS
+    for h in range(SCORE_STEPS):
         some = slice(part * h, part * (h + 1))
         for o in [*xs, x]:
             these = pl.ds(pl.multiple_of(o * block, block), block)
@@ -219,7 +219,7 @@
             scores[h, o] += nt(proj_b[some], weighted[these, cut:]) + nn(norm3[some], hot3)
             if o is not x:
                 send(scores.at[h, o], rx.at[h, x], x_sem.at[h, x], at_x(o))
-    for h in range(STEPS):
+    for h in range(SCORE_STEPS):
         for o in xs:
             arrived(rx.at[h, o], x_sem.at[h, o])
         score = scores[h, x]
@@ -227,9 +227,9 @@
             score += rx[h, o]
         ry[h, 0] = score
         send(ry.at[h, 0], ry.at[h, 1], y_sem.at[h], other_far)
-    for h in range(STEPS):
+    for h in range(SCORE_STEPS):
         arrived(ry.at[h, 1], y_sem.at[h])
-    score = jnp.concatenate([ry[h, 0] + ry[h, 1] for h in range(STEPS)], axis=0) + bias
+    score = jnp.concatenate([ry[h, 0] + ry[h, 1] for h in range(SCORE_STEPS)], axis=0) + bias
 
     high = jnp.max(score, axis=0, keepdims=True)
     raised = jnp.exp(score - high)
@@ -273,7 +273,7 @@
     for o in zs:
         send(s1a.at[o], r1a.at[z], p1a_sem.at[z], at_z(o))
 
-    for h in range(1, STEPS):
+    for h in range(1, SUM_STEPS):
         first_sum_b(h)
 
     by_row = jnp.sum(members.astype(F32), axis=1, keepdims=True)
@@ -293,7 +293,7 @@
             acc += r1b[h, o].astype(F32)
         tb[:zrows, :] = acc
         for o in range(NZ):
-            s2b[h, o] = tb[rows * o : rows * o + 8, :].astype(BF16)
+            s2b[h, o] = tb[rows * o : rows * (o + 1), :].astype(BF16)
         for o in zs:
             send(s2b.at[h, o], r2b.at[h, z], p2b_sem.at[h, z], at_z(o))
 
@@ -311,7 +311,7 @@
 
     second_sum_b(0)
     second_sum_a()
-    for h in range(1, STEPS):
+    for h in range(1, SUM_STEPS):
         second_sum_b(h)
 
     for o in zs:
@@ -342,22 +342,23 @@
     mass_c[0] = mass
     send(mass_c.at[0], mass_c.at[1], mc_sem, other_core)
     arrived(mass_c.at[1], mc_sem)
-    mass_ref[...] = (mass_c[0] + mass_c[1])[0:1] * (logp.shape[1] / (parts * NZ * NY * NC))
-
-    for h in range(STEPS):
+    mass = (mass_c[0] + mass_c[1])[0] * (logp.shape[1] / (parts * NZ * NY * NC))
+    mass_ref[...] = mass
+
+    for h in range(SUM_STEPS):
         for o in zs:
             arrived(r2b.at[h, o], p2b_sem.at[h, o])
         acc = s2b[h, z].astype(F32)
         for o in zs:
             acc += r2b[h, o].astype(F32)
         columns = slice(width * h, width * (h + 1))
-        out_ref[:, first_z + width * h : first_z + width * (h + 1)] = (acc * inverse[:, columns])[:rows]
+        out_ref[:, first_z + width * h : first_z + width * (h + 1)] = acc * inverse[:rows, columns]
 
     for copy in sent:
         copy.wait_send()
 
 
-SENDS = STEPS * (5 * (NZ - 1) + 5 * (NY - 1) + 2 * (NX - 1) + 6)
+SENDS = max(SCORE_STEPS, SUM_STEPS) * (5 * (NZ - 1) + 5 * (NY - 1) + 2 * (NX - 1) + 6)
 
 
 def body(images, ctf_group, projections, ctf_table, noise_power, prior, log_prior, projection_class):
@@ -366,7 +367,7 @@
     classes = log_prior.shape[0]
     rows = projections.shape[0]
     cut, first_z = GATHER_Z, SUM_Z
-    width = (pixels - first_z) // STEPS
+    width = (pixels - first_z) // SUM_STEPS
     krows = NZ * NY * rows
     zrows, yrows = NZ * rows, NY * rows
     chip = NC * parts
@@ -382,7 +383,7 @@
         kernel,
         out_shape=(
             jax.ShapeDtypeStruct((rows, pixels), F32),
-            jax.ShapeDtypeStruct((1, classes), F32),
+            jax.ShapeDtypeStruct((classes,), F32),
         ),
         in_specs=[pl.BlockSpec(memory_space=pl.ANY)] * 8,
         out_specs=[pl.BlockSpec(memory_space=pltpu.VMEM)] * 2,
@@ -406,21 +407,21 @@
             vmem((2 * groups, pixels), BF16),
             vmem((chip, pixels), BF16),
             vmem((NX, groups, block), BF16),
-            vmem((STEPS, NX, krows // STEPS, block), F32),
-            vmem((STEPS, NX, krows // STEPS, block), F32),
-            vmem((STEPS, 2, krows // STEPS, block), F32),
+            vmem((SCORE_STEPS, NX, krows // SCORE_STEPS, block), F32),
+            vmem((SCORE_STEPS, NX, krows // SCORE_STEPS, block), F32),
+            vmem((SCORE_STEPS, 2, krows // SCORE_STEPS, block), F32),
             vmem((2, 8, block), F32),
             vmem((NX, krows, block), BF16),
             vmem((NZ, yrows, first_z + groups), BF16),
-            vmem((STEPS, NY, zrows, width), BF16),
+            vmem((SUM_STEPS, NY, zrows, width), BF16),
             vmem((NZ, yrows, first_z + groups), BF16),
-            vmem((STEPS, NY, zrows, width), BF16),
+            vmem((SUM_STEPS, NY, zrows, width), BF16),
             vmem((up(rows * (NY - 1) + 8), first_z + groups), F32),
             vmem((up(rows * (NZ - 1) + 8), width), F32),
             vmem((NY, 8, first_z + groups), BF16),
-            vmem((STEPS, NZ, 8, width), BF16),
+            vmem((SUM_STEPS, NZ, rows, width), BF16),
             vmem((NY, 8, first_z + groups), BF16),
-            vmem((STEPS, NZ, 8, width), BF16),
+            vmem((SUM_STEPS, NZ, rows, width), BF16),
             vmem((2, 8, classes), F32),
             vmem((NZ, 8, classes), F32),
             vmem((NY, 8, classes), F32),
@@ -428,8 +429,8 @@
             dma((SENDS,)),
             dma, dma,
             dma((NZ,)), dma((NY,)), dma((NY,)), dma((NZ,)),
-            dma((STEPS, NX)), dma((STEPS,)), dma, dma((NX,)),
-            dma((NZ,)), dma((STEPS, NY)), dma((NY,)), dma((STEPS, NZ)),
+            dma((SCORE_STEPS, NX)), dma((SCORE_STEPS,)), dma, dma((NX,)),
+            dma((NZ,)), dma((SUM_STEPS, NY)), dma((NY,)), dma((SUM_STEPS, NZ)),
             dma, dma((NZ,)), dma((NY,)),
         ],
         compiler_params=pltpu.CompilerParams(
@@ -448,7 +449,7 @@
         log_prior.reshape(1, classes),
         projection_class,
     )
-    return sums, mass.reshape(classes)
+    return sums, mass
 
 
 def solution(mesh):

time: 70.5 us -> 70.5 us (level)
  no operation moved by 1% of the time
where the time goes in v3:
time: 70.5 us; the launch traced here: 70.3 us
  Pallas kernels  67.6 us (96%)
  local copies, waits for them, and re-layouts  1.99 us (3%)
    pallas_call x1, Pallas kernels, body(): pl.pallas_call(kernel, out_shape=(jax.ShapeDtypeStruct((rows, pixels), F3...  67.6 us
    unnamed x4, local copies, waits for them, and re-layouts  1.99 us

profile of v3, /device:TPU:1, one launch (start us, length us, event | category | flops | bytes accessed | tf_op | source)
XLA Modules:
  0.0 70.3 jit_solution(18301390948904812235)
XLA Ops:
  0.6 67.6 %shard_map.95 = (f32[6,2048]{1,0:T(8,128)}, f32[16]{0:T(128)}) custom-call(bf16[256,2048]{1,0:T(8,128)(2,1)} %images_hbm.1, s32[1,256]{1,0:T(1,128)} %bitcast.6, bf16[6,2048]{1,0:T(8,128)(2,1)} %proj_hbm.1, f32[128,2048]{1,0:T(8,128)} %ctf_hbm.1, f32[1,2048]{1,0:T(1,128)} %bitcast.4, f32[1,2048]{1,0:T(1,128)} %bitcast.5, f32[1,16]{1,0:T(1,128)} %bitcast.7, ...), custom_call_target="tpu_custom_call" | custom-call | flops 805306368 | bytes 2097152 | tf_op jit(solution)/shard_map/pallas_call | solution.py:382
  68.3 0.0 copy-start
  68.3 1.5 %copy.12 = f32[6,2048]{1,0:T(8,128)} copy(f32[6,2048]{1,0:T(8,128)} %get-tuple-element.4) | data formatting | bytes 98304
  69.8 0.0 copy-done
  69.8 0.5 copy.13
Async XLA Ops:
  68.3 1.5 %copy-start = (f32[16]{0:T(128)S(1)}, f32[16]{0:T(128)}, u32[]{:S(2)}) copy-start(f32[16]{0:T(128)} %get-tuple-element.5) | copy-start | bytes 196

commit v4 on v3

--- a/solution.py
+++ b/solution.py
@@ -67,6 +67,9 @@
     def at_x(o):
         return (dom, o * NF + far)
 
+    def at_x_other(o):
+        return ((y * NZ + z) * NC + (1 - core), o * NF + far)
+
     other_core = ((y * NZ + z) * NC + (1 - core), pix)
     other_far = (dom, x * NF + (1 - far))
     zs = [(z + d) % NZ for d in (4, 3, 5, 2, 6, 1, 7)[8 - NZ :]]
@@ -116,7 +119,7 @@
 
     barrier = pltpu.get_barrier_semaphore()
     peers = [at_z(o) for o in zs] + [at_y(o) for o in ys] + [at_x(o) for o in xs]
-    peers += [other_core, other_far]
+    peers += [at_x_other(o) for o in xs] + [other_core, other_far]
     for peer in peers:
         pl.semaphore_signal(barrier, inc=1, device_id=peer, device_id_type=MESH)
     for copy in loads[:3]:
@@ -234,20 +237,30 @@
     high = jnp.max(score, axis=0, keepdims=True)
     raised = jnp.exp(score - high)
     part = jnp.sum(raised, axis=0, keepdims=True)
-    stats[0, 0:1] = high
-    stats[0, 1:2] = part
-    send(stats.at[0], stats.at[1], st_sem, other_core)
-    arrived(stats.at[1], st_sem)
-    high_o, part_o = stats[1, 0:1], stats[1, 1:2]
-    top = jnp.maximum(high, high_o)
-    scale = jnp.exp(high - top)
-    scale = scale / (part * scale + part_o * jnp.exp(high_o - top))
-    member[x] = (raised * scale).astype(BF16)
+    stats[x, core, 0:1] = high
+    stats[x, core, 1:2] = part
+    mine_st = stats.at[x, core]
+    send(mine_st, mine_st, st_sem.at[x, core], other_core)
+    for o in xs:
+        send(mine_st, mine_st, st_sem.at[x, core], at_x(o))
+        send(mine_st, mine_st, st_sem.at[x, core], at_x_other(o))
+    member[x] = raised.astype(BF16)
     for o in xs:
         send(member.at[x], member.at[x], m_sem.at[x], at_x(o))
+    arrived(stats.at[x, 1 - core], st_sem.at[x, 1 - core])
     for o in xs:
+        arrived(stats.at[o, core], st_sem.at[o, core])
+        arrived(stats.at[o, 1 - core], st_sem.at[o, 1 - core])
         arrived(member.at[o], m_sem.at[o])
-    members = jnp.concatenate([member[o] for o in range(NX)], axis=1)
+    scaled = []
+    for o in range(NX):
+        high, part = stats[o, core, 0:1], stats[o, core, 1:2]
+        high_o, part_o = stats[o, 1 - core, 0:1], stats[o, 1 - core, 1:2]
+        top = jnp.maximum(high, high_o)
+        scale = jnp.exp(high - top)
+        scale = scale / (part * scale + part_o * jnp.exp(high_o - top))
+        scaled.append((member[o].astype(F32) * scale).astype(BF16))
+    members = jnp.concatenate(scaled, axis=1)
 
     def first_sum_b(h):
         columns = slice(first_z + width * h, first_z + width * (h + 1))
@@ -410,7 +423,7 @@
             vmem((SCORE_STEPS, NX, krows // SCORE_STEPS, block), F32),
             vmem((SCORE_STEPS, NX, krows // SCORE_STEPS, block), F32),
             vmem((SCORE_STEPS, 2, krows // SCORE_STEPS, block), F32),
-            vmem((2, 8, block), F32),
+            vmem((NX, NC, 8, block), F32),
             vmem((NX, krows, block), BF16),
             vmem((NZ, yrows, first_z + groups), BF16),
             vmem((SUM_STEPS, NY, zrows, width), BF16),
@@ -429,7 +442,7 @@
             dma((SENDS,)),
             dma, dma,
             dma((NZ,)), dma((NY,)), dma((NY,)), dma((NZ,)),
-            dma((SCORE_STEPS, NX)), dma((SCORE_STEPS,)), dma, dma((NX,)),
+            dma((SCORE_STEPS, NX)), dma((SCORE_STEPS,)), dma((NX, NC)), dma((NX,)),
             dma((NZ,)), dma((SUM_STEPS, NY)), dma((NY,)), dma((SUM_STEPS, NZ)),
             dma, dma((NZ,)), dma((NY,)),
         ],

time: 70.5 us -> 71 us (level)
  no operation moved by 1% of the time
where the time goes in v4:
time: 71 us; the launch traced here: 70.8 us
  Pallas kernels  68.1 us (96%)
  local copies, waits for them, and re-layouts  1.99 us (3%)
    pallas_call x1, Pallas kernels, body(): pl.pallas_call(kernel, out_shape=(jax.ShapeDtypeStruct((rows, pixels), F3...  68.1 us
    unnamed x4, local copies, waits for them, and re-layouts  1.99 us

profile of v4, /device:TPU:1, one launch (start us, length us, event | category | flops | bytes accessed | tf_op | source)
XLA Modules:
  0.0 70.8 jit_solution(2120618848765108487)
XLA Ops:
  0.6 68.1 %shard_map.95 = (f32[6,2048]{1,0:T(8,128)}, f32[16]{0:T(128)}) custom-call(bf16[256,2048]{1,0:T(8,128)(2,1)} %images_hbm.1, s32[1,256]{1,0:T(1,128)} %bitcast.6, bf16[6,2048]{1,0:T(8,128)(2,1)} %proj_hbm.1, f32[128,2048]{1,0:T(8,128)} %ctf_hbm.1, f32[1,2048]{1,0:T(1,128)} %bitcast.4, f32[1,2048]{1,0:T(1,128)} %bitcast.5, f32[1,16]{1,0:T(1,128)} %bitcast.7, ...), custom_call_target="tpu_custom_call" | custom-call | flops 805306368 | bytes 2097152 | tf_op jit(solution)/shard_map/pallas_call | solution.py:395
  68.8 0.0 copy-start
  68.8 1.5 %copy.12 = f32[6,2048]{1,0:T(8,128)} copy(f32[6,2048]{1,0:T(8,128)} %get-tuple-element.4) | data formatting | bytes 98304
  70.3 0.0 copy-done
  70.3 0.5 copy.13
Async XLA Ops:
  68.8 1.5 %copy-start = (f32[16]{0:T(128)S(1)}, f32[16]{0:T(128)}, u32[]{:S(2)}) copy-start(f32[16]{0:T(128)} %get-tuple-element.5) | copy-start | bytes 196

commit v5 on v3

--- a/solution.py
+++ b/solution.py
@@ -311,8 +311,6 @@
 
     second_sum_b(0)
     second_sum_a()
-    for h in range(1, SUM_STEPS):
-        second_sum_b(h)
 
     for o in zs:
         arrived(mass_z.at[o], mz_sem.at[o])
@@ -322,6 +320,9 @@
     mass_y[y] = mass
     for o in ys:
         send(mass_y.at[y], mass_y.at[y], my_sem.at[y], at_y(o))
+
+    for h in range(1, SUM_STEPS):
+        second_sum_b(h)
 
     for o in ys:
         arrived(r2a.at[o], p2a_sem.at[o])

time: 70.5 us -> 70.5 us (level)
  no operation moved by 1% of the time
where the time goes in v5:
time: 70.5 us; the launch traced here: 70.3 us
  Pallas kernels  67.6 us (96%)
  local copies, waits for them, and re-layouts  1.99 us (3%)
    pallas_call x1, Pallas kernels, body(): pl.pallas_call(kernel, out_shape=(jax.ShapeDtypeStruct((rows, pixels), F3...  67.6 us
    unnamed x4, local copies, waits for them, and re-layouts  1.99 us

profile of v5, /device:TPU:1, one launch (start us, length us, event | category | flops | bytes accessed | tf_op | source)
XLA Modules:
  0.0 70.3 jit_solution(16394852928559103631)
XLA Ops:
  0.6 67.6 %shard_map.95 = (f32[6,2048]{1,0:T(8,128)}, f32[16]{0:T(128)}) custom-call(bf16[256,2048]{1,0:T(8,128)(2,1)} %images_hbm.1, s32[1,256]{1,0:T(1,128)} %bitcast.6, bf16[6,2048]{1,0:T(8,128)(2,1)} %proj_hbm.1, f32[128,2048]{1,0:T(8,128)} %ctf_hbm.1, f32[1,2048]{1,0:T(1,128)} %bitcast.4, f32[1,2048]{1,0:T(1,128)} %bitcast.5, f32[1,16]{1,0:T(1,128)} %bitcast.7, ...), custom_call_target="tpu_custom_call" | custom-call | flops 805306368 | bytes 2097152 | tf_op jit(solution)/shard_map/pallas_call | solution.py:383
  68.3 0.0 copy-start
  68.3 1.5 %copy.12 = f32[6,2048]{1,0:T(8,128)} copy(f32[6,2048]{1,0:T(8,128)} %get-tuple-element.4) | data formatting | bytes 98304
  69.8 0.0 copy-done
  69.8 0.5 copy.13
Async XLA Ops:
  68.3 1.5 %copy-start = (f32[16]{0:T(128)S(1)}, f32[16]{0:T(128)}, u32[]{:S(2)}) copy-start(f32[16]{0:T(128)} %get-tuple-element.5) | copy-start | bytes 196
